TPU v7x, 32 devices: a whole 2x2x4 slice. The times are simulated.
32 devices in a mesh: section: 4 (over x, core), dp: 8 (over z, y).
Axes of the slice: x: 2, y: 2, z: 4, core: 2. Of those that a mesh axis runs over, the one named last changes fastest.
Arguments:
- x_enc: bfloat16 [2, 512, 2048], P(None, 'dp'), may hold values from -6 to 6
- x_dec: bfloat16 [2, 512, 2048], P(None, 'dp'), may hold values from -6 to 6
- d_out: bfloat16 [2, 512, 2048], P(None, 'dp'), may hold values from -6 to 6
- lengths: int32 [2, 8], P(None, 'dp'), may hold values from 16 to 64, as said below
- w_query: bfloat16 [4, 2048, 2048], P('section', 'dp'), may hold values from -0.125 to 0.125
- gain: bfloat16 [4, 2048], P('section', 'dp'), may hold values from 0.5 to 1.5
Outputs:
- section_out: bfloat16 [4, 2, 512, 2048], P('section', None, 'dp')
- d_inputs: bfloat16 [4, 2, 512, 2048], P('section', None, 'dp')
- grad_query: float32 [4, 2048, 2048], P('section', 'dp')
- grad_gain: float32 [4, 2048], P('section', 'dp')
Inputs may be any that keep to these rules, and one draw needn't show every extreme that they name: `lengths`: each length is 16 to 64; both ends are taken by some sequence.
All inputs are finite; a program needn't handle non-finite values.
Results may differ from a plain program's by a relative error of at most 0.025.
Values may be sent and summed in bfloat16 or wider, within the bound.
A program may use at most 128 MiB of HBM per device.

v0:
```python
import jax
import jax.numpy as jnp
from jax import lax
from jax.sharding import PartitionSpec as P

HEAD = 256


norm_eps = 1e-06
mix_scale = 4.0


def from_behind(block, axis, distance):
    devices = range(lax.axis_size(axis))
    route = [(i - distance, i) for i in devices if i - distance in devices]
    return lax.ppermute(block, axis, route)


def from_root(value, axis, source):
    kept = jnp.where(lax.axis_index(axis) == source, value, 0).astype(value.dtype)
    return lax.psum(kept, axis)


def contract(left, right, left_dim, right_dim):
    return lax.dot_general(
        left, right, (((left_dim,), (right_dim,)), ((), ())), preferred_element_type=jnp.float32
    )


def normed(values, gain_row):
    squares = jnp.mean(values * values, axis=-1, keepdims=True)
    return (values * lax.rsqrt(squares + norm_eps) * gain_row).astype(jnp.bfloat16)


def prepare(inputs_f32, source_f32, gain_f32):
    return (normed(inputs_f32, gain_f32), normed(source_f32, gain_f32))


def attend(query, keys, source):
    row_count, features = query.shape
    heads = features // HEAD
    score_scale = HEAD ** (-0.5)
    query_heads = query.reshape(row_count, heads, HEAD)
    key_heads = keys.reshape(-1, heads, HEAD)
    value_heads = source.reshape(-1, heads, HEAD)
    scores = (
        jnp.einsum("qhd,khd->hqk", query_heads, key_heads, preferred_element_type=jnp.float32)
        * score_scale
    )
    weights = jnp.exp(scores)
    probs = (weights / jnp.sum(weights, axis=-1, keepdims=True)).astype(jnp.bfloat16)
    mixed = jnp.einsum("hqk,khd->qhd", probs, value_heads, preferred_element_type=jnp.float32)
    return mixed.reshape(row_count, features).astype(jnp.bfloat16)


def forward_layer(layer_input, source, w_query, gain_row):
    normed_query, keys = prepare(
        layer_input.astype(jnp.float32), source.astype(jnp.float32), gain_row.astype(jnp.float32)
    )
    query = jnp.dot(normed_query, w_query, preferred_element_type=jnp.float32).astype(jnp.bfloat16)
    mixed = attend(query, keys, source)
    return (layer_input.astype(jnp.float32) + mix_scale * mixed.astype(jnp.float32)).astype(
        jnp.bfloat16
    )


def backward_layer(layer_input, source, d_result, w_query, gain_row):
    (normed_query, keys), prep_back = jax.vjp(
        prepare,
        layer_input.astype(jnp.float32),
        source.astype(jnp.float32),
        gain_row.astype(jnp.float32),
    )
    query = jnp.dot(normed_query, w_query, preferred_element_type=jnp.float32).astype(jnp.bfloat16)
    mixed, attend_back = jax.vjp(attend, query, keys, source)
    d_mixed = (mix_scale * d_result.astype(jnp.float32)).astype(jnp.bfloat16)
    d_query, d_keys, d_values = attend_back(d_mixed)
    d_normed = contract(d_query, w_query, 1, 1).astype(jnp.bfloat16)
    d_input, d_source, d_gain = prep_back((d_normed, d_keys))
    d_input = d_input + d_result.astype(jnp.float32)
    d_source = d_source + d_values.astype(jnp.float32)
    return (d_input, d_source, d_gain, normed_query, d_query)


def shards(x_enc, x_dec, d_out, lengths, w_query, gain):
    sections = lax.axis_size("section")
    section_num = lax.axis_index("section")
    micro, seq_rows, features = x_enc.shape
    full_query, full_gain = (
        lax.all_gather(w_query, "dp", axis=1, tiled=True),
        lax.all_gather(gain, "dp", axis=1, tiled=True),
    )
    full_query = full_query[0]
    full_gain = full_gain[0]
    row_index = lax.broadcasted_iota(jnp.int32, (micro, seq_rows, 1), 1)
    d_last = jnp.where(row_index < lengths[:, :, None], d_out, jnp.zeros_like(d_out))
    blank_rows = jnp.zeros((seq_rows, features), jnp.bfloat16)
    blank_buffer = jnp.zeros((micro, seq_rows, features), jnp.bfloat16)

    def run_forward(layer_input, source):
        return forward_layer(layer_input, source, full_query, full_gain)

    def skip_forward(layer_input, source):
        return blank_rows

    inputs_buf = blank_buffer
    memories = blank_buffer
    outputs_buf = blank_buffer
    incoming = blank_rows
    for moment in range(micro + sections - 1):
        batch_slot = moment - section_num
        active = (batch_slot >= 0) & (batch_slot < micro)
        slot_index = jnp.clip(batch_slot, 0, micro - 1)
        decoder_start = (
            x_dec[slot_index].astype(jnp.float32) + incoming.astype(jnp.float32)
        ).astype(jnp.bfloat16)
        layer_input = jnp.where(
            section_num == 0,
            x_enc[slot_index],
            jnp.where(section_num == 1, decoder_start, incoming),
        )
        source = jnp.where(section_num == 0, layer_input, memories[slot_index])
        result = lax.cond(active, run_forward, skip_forward, layer_input, source)
        inputs_buf = jnp.where(active, inputs_buf.at[slot_index].set(layer_input), inputs_buf)
        outputs_buf = jnp.where(active, outputs_buf.at[slot_index].set(result), outputs_buf)
        incoming = from_behind(result, "section", 1)
        if moment < micro:
            memories = memories.at[moment].set(from_root(result, "section", 0))

    def run_backward(layer_input, source, d_result):
        return backward_layer(layer_input, source, d_result, full_query, full_gain)

    def skip_backward(layer_input, source, d_result):
        zero_rows = jnp.zeros((seq_rows, features), jnp.float32)
        return (zero_rows, zero_rows, jnp.zeros((features,), jnp.float32), blank_rows, blank_rows)

    d_memory = jnp.zeros((micro, seq_rows, features), jnp.float32)
    d_in_buf = blank_buffer
    normed_buf = blank_buffer
    dquery_buf = blank_buffer
    gain_grad = jnp.zeros((features,), jnp.float32)
    incoming = blank_rows
    is_encoder = section_num == 0
    for moment in range(micro + sections - 2, 0, -1):
        batch_slot = moment - section_num
        active = (batch_slot >= 0) & (batch_slot < micro) & (section_num > 0)
        slot_index = jnp.clip(batch_slot, 0, micro - 1)
        d_result = jnp.where(section_num == sections - 1, d_last[slot_index], incoming)
        parts = lax.cond(
            active,
            run_backward,
            skip_backward,
            inputs_buf[slot_index],
            memories[slot_index],
            d_result,
        )
        d_input = parts[0].astype(jnp.bfloat16)
        d_in_buf = jnp.where(active, d_in_buf.at[slot_index].set(d_input), d_in_buf)
        d_memory = d_memory.at[slot_index].add(parts[1])
        gain_grad = gain_grad + parts[2]
        normed_buf = jnp.where(active, normed_buf.at[slot_index].set(parts[3]), normed_buf)
        dquery_buf = jnp.where(active, dquery_buf.at[slot_index].set(parts[4]), dquery_buf)
        incoming = from_behind(d_input, "section", -1)
        if moment - 1 < micro:
            arrived = jnp.where(
                is_encoder,
                incoming.astype(jnp.float32),
                jnp.zeros((seq_rows, features), jnp.float32),
            )
            d_memory = d_memory.at[moment - 1].add(arrived)
    d_memory = lax.psum(d_memory.astype(jnp.bfloat16), "section").astype(jnp.float32)
    for batch_slot in range(micro):
        layer_input = inputs_buf[batch_slot]
        d_result = d_memory[batch_slot].astype(jnp.bfloat16)
        parts = lax.cond(
            is_encoder, run_backward, skip_backward, layer_input, layer_input, d_result
        )
        d_input = (parts[0] + parts[1]).astype(jnp.bfloat16)
        d_in_buf = jnp.where(is_encoder, d_in_buf.at[batch_slot].set(d_input), d_in_buf)
        gain_grad = gain_grad + parts[2]
        normed_buf = jnp.where(is_encoder, normed_buf.at[batch_slot].set(parts[3]), normed_buf)
        dquery_buf = jnp.where(is_encoder, dquery_buf.at[batch_slot].set(parts[4]), dquery_buf)
    flat_normed = normed_buf.reshape(micro * seq_rows, features)
    flat_dquery = dquery_buf.reshape(micro * seq_rows, features)
    term_query = contract(flat_normed, flat_dquery, 0, 0)
    grad_query, grad_gain = (
        lax.psum_scatter(
            term_query[None].astype(jnp.bfloat16), "dp", scatter_dimension=1, tiled=True
        ).astype(jnp.float32),
        lax.psum_scatter(
            gain_grad[None].astype(jnp.bfloat16), "dp", scatter_dimension=1, tiled=True
        ).astype(jnp.float32),
    )
    return (outputs_buf[None], d_in_buf[None], grad_query, grad_gain)


def solution(mesh):
    in_specs = (
        P(None, "dp", None),
        P(None, "dp", None),
        P(None, "dp", None),
        P(None, "dp"),
        P("section", "dp", None),
        P("section", "dp"),
    )
    out_specs = (
        P("section", None, "dp", None),
        P("section", None, "dp", None),
        P("section", "dp", None),
        P("section", "dp"),
    )
    return jax.shard_map(shards, mesh=mesh, in_specs=in_specs, out_specs=out_specs, check_vma=False)
```

profile of v0, /device:TPU:0, one launch (start us, length us, event | category | flops | bytes accessed | tf_op | source)
XLA Modules:
  0.0 689.9 jit_solution(17042824924697611812)
XLA Ops:
  8.0 22.6 %all_gather.6 = bf16[1,2048]{1,0:T(2,128)(2,1)S(1)} all-gather(bf16[1,256]{1,0:T(2,128)(2,1)} %param.105), channel_id=1, replica_groups=mesh['section'=4,'dp'=8] {'dp'}, dimensions={1}, use_global_device_ids=true | all-gather | bytes 4608 | tf_op jit(solution)/shard_map/all_gather | solution.py:91
  35.3 102.6 %all-gather.2.cloned.1.call-done = bf16[1,2048,2048]{2,1,0:T(8,128)(2,1)} async-done(((bf16[1,256,2048]{2,1,0:T(8,128)(2,1)}), bf16[1,2048,2048]{2,1,0:T(8,128)(2,1)}) %all-gather.2.cloned.1.call-update) | async-done | bytes 8388624 | tf_op jit(solution)/shard_map/all_gather | solution.py:90
  137.9 8.0 %conditional.11 = (bf16[64,2048]{1,0:T(8,128)(2,1)S(1)}) conditional(s32[]{:T(128)} %convert_element_type.1174, () %tuple.316, (pred[]{:T(512)}, bf16[1,64,2048]{2,1,0:T(8,128)(2,1)S(1)}, pred[]{:T(512)}, bf16[1,64,2048]{2,1,0:T(8,128)(2,1)S(1)}, bf16[64,2048]{1,0:T(8,128)(2,1)S(1)}, /*index=5*/bf16[2048]{0:T(1024)(128)(2,1)S(1)}, ...), branch_computations={%region_1.2_spmd, %region_2.6_spmd} | conditional | flops 573672128 | bytes 14972939 | solution.py:123
  138.3 5.0 convolution_convert_fusion
  149.1 28.3 %all-reduce.5.cloned.1.call-done = bf16[1,64,2048]{2,1,0:T(8,128)(2,1)} async-done(((bf16[1,64,2048]{2,1,0:T(8,128)(2,1)}), bf16[1,64,2048]{2,1,0:T(8,128)(2,1)}) %all-reduce.5.cloned.1.call-update) | async-done | bytes 262160 | tf_op jit(solution)/shard_map/psum | solution.py:21
  177.3 7.7 %conditional.12 = (bf16[64,2048]{1,0:T(8,128)(2,1)}, bf16[1,64,2048]{2,1,0:T(8,128)(2,1)S(1)}) conditional(s32[]{:T(128)} %convert_element_type.1175, () %tuple.318, (bf16[64,2048]{1,0:T(8,128)(2,1)S(1)}, bf16[2048]{0:T(1024)(128)(2,1)S(1)}, bf16[2048,2048]{1,0:T(8,128)(2,1)}, pred[]{:T(512)}, bf16[1,64,2048]{2,1,0:T(8,128)(2,1)}, ...), branch_computations={%region_8.9_spmd, %region_9.13_spmd} | conditional | flops 573409984 | bytes 14448661 | solution.py:123
  177.6 5.0 convolution_convert_fusion.2
  189.2 29.8 %all-reduce.7.cloned.1.call-done = bf16[1,64,2048]{2,1,0:T(8,128)(2,1)} async-done(((bf16[1,64,2048]{2,1,0:T(8,128)(2,1)}), bf16[1,64,2048]{2,1,0:T(8,128)(2,1)}) %all-reduce.7.cloned.1.call-update) | async-done | bytes 262160 | tf_op jit(solution)/shard_map/psum | solution.py:21
  223.4 10.1 %collective-permute-start.2 = (bf16[64,2048]{1,0:T(8,128)(2,1)}, bf16[64,2048]{1,0:T(8,128)(2,1)S(1)}, u32[]{:S(2)}, u32[]{:S(2)}) collective-permute-start(bf16[64,2048]{1,0:T(8,128)(2,1)} %get-tuple-element.1083), channel_id=1, source_target_pairs={{0,8},{8,16},{16,24},{1,9},{9,17},{17,25},{2,10},{10,18},{18,26},{... | collective-permute-start | bytes 786440 | tf_op jit(solution)/shard_map/ppermute | solution.py:16
  236.5 6.0 collective-permute-start.3
  245.4 2.5 conditional.16
  253.6 12.7 %collective-permute-done.4 = bf16[64,2048]{1,0:T(8,128)(2,1)S(1)} collective-permute-done((bf16[64,2048]{1,0:T(8,128)(2,1)}, bf16[64,2048]{1,0:T(8,128)(2,1)S(1)}, u32[]{:S(2)}, u32[]{:S(2)}) %collective-permute-start.4) | collective-permute-done | bytes 262176 | tf_op jit(solution)/shard_map/ppermute | solution.py:16
  266.2 3.0 conditional.17
  274.7 2.4 fusion.411
  278.5 12.7 %conditional.18 = (f32[2048]{0:T(1024)S(1)}, bf16[64,2048]{1,0:T(8,128)(2,1)}, bf16[1,64,2048]{2,1,0:T(8,128)(2,1)S(1)}, f32[1,64,2048]{2,1,0:T(8,128)}, bf16[1,...) conditional(s32[]{:T(128)} %convert_element_type.1197, () %tuple.330, (bf16[64,2048]{1,0:T(8,128)(2,1)S(1)}, ...), branch_computations={%region_52.53_spmd, %region_53.62_spmd} | conditional | flops 1166181632 | bytes 39449840 | solution.py:149
  296.5 2.4 fusion.412
  298.9 44.7 %collective-permute-done.6 = bf16[64,2048]{1,0:T(8,128)(2,1)S(1)} collective-permute-done((bf16[64,2048]{1,0:T(8,128)(2,1)}, bf16[64,2048]{1,0:T(8,128)(2,1)S(1)}, u32[]{:S(2)}, u32[]{:S(2)}) %collective-permute-start.6) | collective-permute-done | bytes 262176 | tf_op jit(solution)/shard_map/ppermute | solution.py:16
  343.6 2.3 conditional.19
  350.7 38.6 %collective-permute-done.7 = bf16[64,2048]{1,0:T(8,128)(2,1)S(1)} collective-permute-done((bf16[64,2048]{1,0:T(8,128)(2,1)}, bf16[64,2048]{1,0:T(8,128)(2,1)S(1)}, u32[]{:S(2)}, u32[]{:S(2)}) %collective-permute-start.7) | collective-permute-done | bytes 262176 | tf_op jit(solution)/shard_map/ppermute | solution.py:16
  390.4 2.3 fusion.413
  392.6 35.8 %all-reduce.9.cloned.1.call-done = bf16[2,64,2048]{2,1,0:T(8,128)(2,1)} async-done(((bf16[2,64,2048]{2,1,0:T(8,128)(2,1)}), bf16[2,64,2048]{2,1,0:T(8,128)(2,1)}) %all-reduce.9.cloned.1.call-update) | async-done | bytes 524304 | tf_op jit(solution)/shard_map/psum | solution.py:171
  428.4 16.3 %conditional.21 = (f32[64,2048]{1,0:T(8,128)}, f32[64,2048]{1,0:T(8,128)S(1)}, f32[2048]{0:T(1024)S(1)}, bf16[1,64,2048]{2,1,0:T(8,128)(2,1)}, bf16[1,64,2048]{2,1,0:T(8,128)(2,1)}) conditional(s32[]{:T(128)} %convert_element_type.1199, () %tuple.336, (bf16[2,64,2048]{2,1,0:T(8,128)(2,1)}, bf16[2,64,2048]{2,1,0:T(8,128)(2,1)S(1)}, ...), branch_computations={%region_82.83_spmd, %region_83.91_spmd} | conditional | flops 1165001728 | bytes 35525700 | solution.py:175
  428.8 5.1 convolution_convert_fusion.41
  437.4 6.2 fusion.360
  445.5 19.0 %conditional.20 = (f32[64,2048]{1,0:T(8,128)}, f32[64,2048]{1,0:T(8,128)}, f32[2048]{0:T(1024)S(1)}, bf16[1,64,2048]{2,1,0:T(8,128)(2,1)}, bf16[1,64,2048]{2,1,0:T(8,128)(2,1)}) conditional(s32[]{:T(128)} %convert_element_type.1199, () %tuple.334, (bf16[2,64,2048]{2,1,0:T(8,128)(2,1)}, bf16[2,64,2048]{2,1,0:T(8,128)(2,1)S(1)}, ...), branch_computations={%region_73.74_spmd, %region_74.82_spmd} | conditional | flops 1165001728 | bytes 36574304 | solution.py:175
  445.7 5.1 convolution_convert_fusion.35
  457.0 6.2 fusion.316
  469.5 5.6 fusion.385
  483.5 1.9 fusion.403
  485.4 42.5 %reduce-scatter.7.cloned.1.call-done = bf16[256,1]{1,0:T(8,128)(2,1)} async-done(((bf16[2048,1]{1,0:T(8,128)(2,1)}), bf16[256,1]{1,0:T(8,128)(2,1)}) %reduce-scatter.7.cloned.1.call-update) | async-done | bytes 528
  529.4 150.5 %reduce-scatter.5.cloned.1.call-done = bf16[1,256,2048]{2,1,0:T(8,128)(2,1)} async-done(((bf16[1,2048,2048]{2,1,0:T(8,128)(2,1)}), bf16[1,256,2048]{2,1,0:T(8,128)(2,1)}) %reduce-scatter.5.cloned.1.call-update) | async-done | bytes 1048592 | tf_op jit(solution)/shard_map/reduce_scatter | solution.py:187
  679.9 2.8 convert_element_type.1208
  (250 shorter events, 91.8 us)
Async XLA Ops:
  7.2 130.6 %all-gather.2.cloned.1.call-start = ((), (), s32[]{:S(2)}) async-start(), calls=%async_computation.2 | async-start | bytes 9437184 | tf_op jit(solution)/shard_map/all_gather | solution.py:90
  7.9 169.4 %all-reduce.5.cloned.1.call-start = ((), (), s32[]{:S(2)}) async-start(), calls=%async_computation.3 | async-start | bytes 524288 | tf_op jit(solution)/shard_map/psum | solution.py:21
  137.8 10.5 %copy-start.6 = (bf16[2,64,2048]{2,1,0:T(8,128)(2,1)S(1)}, bf16[2,64,2048]{2,1,0:T(8,128)(2,1)}, u32[]{:S(2)}) copy-start(bf16[2,64,2048]{2,1,0:T(8,128)(2,1)} %param.100) | copy-start | bytes 1572868
  137.8 10.5 %copy-start.7 = (bf16[2,64,2048]{2,1,0:T(8,128)(2,1)S(1)}, bf16[2,64,2048]{2,1,0:T(8,128)(2,1)}, u32[]{:S(2)}) copy-start(bf16[2,64,2048]{2,1,0:T(8,128)(2,1)} %param.101) | copy-start | bytes 1572868
  145.9 31.5 %copy-start.8 = (bf16[64,2048]{1,0:T(8,128)(2,1)}, bf16[64,2048]{1,0:T(8,128)(2,1)S(1)}, u32[]{:S(2)}) copy-start(bf16[64,2048]{1,0:T(8,128)(2,1)S(1)} %get-tuple-element.1341) | copy-start | bytes 786436
  145.9 2.4 collective-permute-start
  147.9 71.0 %all-reduce.7.cloned.1.call-start = ((), (), s32[]{:S(2)}) async-start(), calls=%async_computation.4 | async-start | bytes 524288 | tf_op jit(solution)/shard_map/psum | solution.py:21
  186.8 241.6 %all-reduce.9.cloned.1.call-start = ((), (), s32[]{:S(2)}) async-start(), calls=%async_computation.5 | async-start | bytes 1048576 | tf_op jit(solution)/shard_map/psum | solution.py:171
  187.9 32.2 %collective-permute-start.1 = (bf16[64,2048]{1,0:T(8,128)(2,1)}, bf16[64,2048]{1,0:T(8,128)(2,1)S(1)}, u32[]{:S(2)}, u32[]{:S(2)}) collective-permute-start(bf16[64,2048]{1,0:T(8,128)(2,1)} %get-tuple-element.1081), channel_id=1, source_target_pairs={{0,8},{8,16},{16,24},{1,9},{9,17},{17,25},{2,10},{10,18},{18,26},{... | collective-permute-start | bytes 786440 | tf_op jit(solution)/shard_map/ppermute | solution.py:16
  222.7 10.9 %copy-start.56 = (s32[2,1]{0,1:T(1,128)S(1)}, s32[2,1]{0,1:T(1,128)}, u32[]{:S(2)}) copy-start(s32[2,1]{0,1:T(1,128)} %param.103) | copy-start | bytes 28
  223.4 11.4 %copy-start.33 = (bf16[1,64,2048]{2,1,0:T(8,128)(2,1)}, bf16[1,64,2048]{2,1,0:T(8,128)(2,1)S(1)}, u32[]{:S(2)}) copy-start(bf16[1,64,2048]{2,1,0:T(8,128)(2,1)S(1)} %get-tuple-element.1082) | copy-start | bytes 786436
  223.4 11.4 %collective-permute-start.2 = (bf16[64,2048]{1,0:T(8,128)(2,1)}, bf16[64,2048]{1,0:T(8,128)(2,1)S(1)}, u32[]{:S(2)}, u32[]{:S(2)}) collective-permute-start(bf16[64,2048]{1,0:T(8,128)(2,1)} %get-tuple-element.1083), channel_id=1, source_target_pairs={{0,8},{8,16},{16,24},{1,9},{9,17},{17,25},{2,10},{10,18},{18,26},{... | collective-permute-start | bytes 786440 | tf_op jit(solution)/shard_map/ppermute | solution.py:16
  236.5 9.0 %copy-start.35 = (bf16[1,64,2048]{2,1,0:T(8,128)(2,1)}, bf16[1,64,2048]{2,1,0:T(8,128)(2,1)S(1)}, u32[]{:S(2)}) copy-start(bf16[1,64,2048]{2,1,0:T(8,128)(2,1)S(1)} %get-tuple-element.1084) | copy-start | bytes 786436
  236.5 7.3 %collective-permute-start.3 = (bf16[64,2048]{1,0:T(8,128)(2,1)}, bf16[64,2048]{1,0:T(8,128)(2,1)S(1)}, u32[]{:S(2)}, u32[]{:S(2)}) collective-permute-start(bf16[64,2048]{1,0:T(8,128)(2,1)} %get-tuple-element.1085), channel_id=1, source_target_pairs={{0,8},{8,16},{16,24},{1,9},{9,17},{17,25},{2,10},{10,18},{18,26},{... | collective-permute-start | bytes 786440 | tf_op jit(solution)/shard_map/ppermute | solution.py:16
  247.9 18.3 %collective-permute-start.4 = (bf16[64,2048]{1,0:T(8,128)(2,1)}, bf16[64,2048]{1,0:T(8,128)(2,1)S(1)}, u32[]{:S(2)}, u32[]{:S(2)}) collective-permute-start(bf16[64,2048]{1,0:T(8,128)(2,1)} %get-tuple-element.1086), channel_id=1, source_target_pairs={{8,0},{16,8},{24,16},{9,1},{17,9},{25,17},{10,2},{18,10},{26,18},{... | collective-permute-start | bytes 786440 | tf_op jit(solution)/shard_map/ppermute | solution.py:16
  253.6 12.7 %copy-start = (bf16[2,64,2048]{2,1,0:T(8,128)(2,1)}, bf16[2,64,2048]{2,1,0:T(8,128)(2,1)S(1)}, u32[]{:S(2)}) copy-start(bf16[2,64,2048]{2,1,0:T(8,128)(2,1)S(1)} %bitcast_dynamic-update-slice_fusion.2) | copy-start | bytes 1572868
  270.0 8.5 %collective-permute-start.5 = (bf16[64,2048]{1,0:T(8,128)(2,1)}, bf16[64,2048]{1,0:T(8,128)(2,1)S(1)}, u32[]{:S(2)}, u32[]{:S(2)}) collective-permute-start(bf16[64,2048]{1,0:T(8,128)(2,1)} %get-tuple-element.1088), channel_id=1, source_target_pairs={{8,0},{16,8},{24,16},{9,1},{17,9},{25,17},{10,2},{18,10},{26,18},{... | collective-permute-start | bytes 786440 | tf_op jit(solution)/shard_map/ppermute | solution.py:16
  291.8 51.9 %copy-start.27 = (bf16[1,64,2048]{2,1,0:T(8,128)(2,1)}, bf16[1,64,2048]{2,1,0:T(8,128)(2,1)S(1)}, u32[]{:S(2)}) copy-start(bf16[1,64,2048]{2,1,0:T(8,128)(2,1)S(1)} %get-tuple-element.1089) | copy-start | bytes 786436
  291.8 51.9 %collective-permute-start.6 = (bf16[64,2048]{1,0:T(8,128)(2,1)}, bf16[64,2048]{1,0:T(8,128)(2,1)S(1)}, u32[]{:S(2)}, u32[]{:S(2)}) collective-permute-start(bf16[64,2048]{1,0:T(8,128)(2,1)} %get-tuple-element.1090), channel_id=1, source_target_pairs={{8,0},{16,8},{24,16},{9,1},{17,9},{25,17},{10,2},{18,10},{26,18},{... | collective-permute-start | bytes 786440 | tf_op jit(solution)/shard_map/ppermute | solution.py:16
  346.0 82.4 %copy-start.44 = (f32[2048]{0:T(1024)}, f32[2048]{0:T(1024)S(1)}, u32[]{:S(2)}) copy-start(f32[2048]{0:T(1024)S(1)} %get-tuple-element.1116) | copy-start | bytes 24580
  346.0 82.4 %copy-start.29 = (bf16[1,64,2048]{2,1,0:T(8,128)(2,1)}, bf16[1,64,2048]{2,1,0:T(8,128)(2,1)S(1)}, u32[]{:S(2)}) copy-start(bf16[1,64,2048]{2,1,0:T(8,128)(2,1)S(1)} %get-tuple-element.1091) | copy-start | bytes 786436
  346.0 43.3 %collective-permute-start.7 = (bf16[64,2048]{1,0:T(8,128)(2,1)}, bf16[64,2048]{1,0:T(8,128)(2,1)S(1)}, u32[]{:S(2)}, u32[]{:S(2)}) collective-permute-start(bf16[64,2048]{1,0:T(8,128)(2,1)} %get-tuple-element.1096), channel_id=1, source_target_pairs={{8,0},{16,8},{24,16},{9,1},{17,9},{25,17},{10,2},{18,10},{26,18},{... | collective-permute-start | bytes 786440 | tf_op jit(solution)/shard_map/ppermute | solution.py:16
  390.3 137.6 %reduce-scatter.7.cloned.1.call-start = ((), (), s32[]{:S(2)}) async-start(), calls=%async_computation.7 | async-start | bytes 589824
  444.7 19.8 %copy-start.41 = (f32[2048]{0:T(1024)S(1)}, f32[2048]{0:T(1024)}, u32[]{:S(2)}) copy-start(f32[2048]{0:T(1024)} %copy-done.40) | copy-start | bytes 24580
  444.7 19.8 %copy-start.43 = (f32[2048]{0:T(1024)S(1)}, f32[2048]{0:T(1024)}, u32[]{:S(2)}) copy-start(f32[2048]{0:T(1024)} %copy-done.42) | copy-start | bytes 24580
  444.7 19.8 %copy-start.45 = (f32[2048]{0:T(1024)S(1)}, f32[2048]{0:T(1024)}, u32[]{:S(2)}) copy-start(f32[2048]{0:T(1024)} %copy-done.44) | copy-start | bytes 24580
  444.7 19.8 %copy-start.47 = (f32[2048]{0:T(1024)S(1)}, f32[2048]{0:T(1024)}, u32[]{:S(2)}) copy-start(f32[2048]{0:T(1024)} %copy-done.46) | copy-start | bytes 24580
  444.7 22.4 %copy-start.1 = (bf16[2,64,2048]{2,1,0:T(8,128)(2,1)S(1)}, bf16[2,64,2048]{2,1,0:T(8,128)(2,1)}, u32[]{:S(2)}) copy-start(bf16[2,64,2048]{2,1,0:T(8,128)(2,1)} %fusion.413) | copy-start | bytes 1572868
  465.8 214.1 %reduce-scatter.5.cloned.1.call-start = ((), (), s32[]{:S(2)}) async-start(), calls=%async_computation.6 | async-start | bytes 9437184 | tf_op jit(solution)/shard_map/reduce_scatter | solution.py:187
  469.5 7.8 %copy-start.36 = (bf16[1,64,2048]{2,1,0:T(8,128)(2,1)S(1)}, bf16[1,64,2048]{2,1,0:T(8,128)(2,1)}, u32[]{:S(2)}) copy-start(bf16[1,64,2048]{2,1,0:T(8,128)(2,1)} %copy-done.35) | copy-start | bytes 786436
  485.4 197.3 %copy-start.37 = (bf16[1,2,64,2048]{3,2,1,0:T(8,128)(2,1)}, bf16[1,2,64,2048]{3,2,1,0:T(8,128)(2,1)S(1)}, u32[]{:S(2)}) copy-start(bf16[1,2,64,2048]{3,2,1,0:T(8,128)(2,1)S(1)} %get-tuple-element.1261) | copy-start | bytes 1572868
  485.4 197.3 %copy-start.38 = (bf16[1,2,64,2048]{3,2,1,0:T(8,128)(2,1)}, bf16[1,2,64,2048]{3,2,1,0:T(8,128)(2,1)S(1)}, u32[]{:S(2)}) copy-start(bf16[1,2,64,2048]{3,2,1,0:T(8,128)(2,1)S(1)} %get-tuple-element.1262) | copy-start | bytes 1572868
  (19 other events, 59.0 us)
Sparse Core Ops, SparseCore 0:
  10.1 127.6 all-gather.1
  148.0 29.2 all-reduce.4
  186.9 31.9 all-reduce.6
  390.4 37.9 all-reduce.8
  465.9 61.9 reduce-scatter.6
  531.8 147.9 reduce-scatter.4
where the time goes:
time: 700 us; the launch traced here: 690 us
  waiting for transfers between devices  489 us (70%)
  other arithmetic  58.9 us (8%)
  matrix products  43.3 us (6%)
  local copies, waits for them, and re-layouts  25.9 us (4%)
  starting transfers between devices  24.3 us (3%)
  blocking collectives  22.6 us (3%)
  between operations  15.3 us (2%)
  loops' own time  10.6 us (2%)
    reduce_scatter x1, waiting for transfers between devices, shards(): lax.psum_scatter(term_query[None].astype(jnp.bfloat16), 'dp', scatter_dim...  150 us
    all_gather x1, waiting for transfers between devices, shards(): lax.all_gather(w_query, 'dp', axis=1, tiled=True)  103 us
    ppermute x8, waiting for transfers between devices, from_behind(): return lax.ppermute(block, axis, route)  99.1 us
    psum x2, waiting for transfers between devices, from_root(): return lax.psum(kept, axis)  58 us
    unnamed x7, waiting for transfers between devices  43.3 us
    psum x1, waiting for transfers between devices, shards(): lax.psum(d_memory.astype(jnp.bfloat16), 'section').astype(jnp.float32)  35.8 us
    ppermute x8, starting transfers between devices, from_behind(): return lax.ppermute(block, axis, route)  23.8 us
    all_gather x1, blocking collectives, shards(): lax.all_gather(gain, 'dp', axis=1, tiled=True)  22.6 us
  transfers between devices with their start and end apart: 14, of which 13 were waited for; matrix products, arithmetic and copies ran while one was open for 7% of the time, Pallas kernels for 0%

commit v1 on v0

v1 whole, which is shorter than its diff:
```python
import functools

import jax
import jax.numpy as jnp
from jax import lax
from jax.experimental import pallas as pl
from jax.experimental.pallas import tpu as pltpu
from jax.sharding import PartitionSpec as P

HEAD = 256
norm_eps = 1e-06
mix_scale = 4.0
TAIL = 128
F32, BF16 = jnp.float32, jnp.bfloat16


def dot(left, right, left_dim, right_dim):
    return lax.dot_general(
        left, right, (((left_dim,), (right_dim,)), ((), ())), preferred_element_type=F32
    )


def inv_norm(chunks, features):
    total = sum(jnp.sum(c * c, axis=-1, keepdims=True) for c in chunks)
    return lax.rsqrt(total * (1.0 / features) + norm_eps)


def softmax_parts(query, keys):
    weights = jnp.exp(dot(query, keys, 1, 1) * HEAD ** (-0.5))
    return weights / jnp.sum(weights, axis=-1, keepdims=True)


def cascade_kernel(
    n, micro, x_enc, x_dec, d_last, weights, gain,
    out_ref, din_ref, nq_ref, dq_ref, dg_ref,
    y_buf, x_one, p_send, p_recv, d_own, d_recv, q_buf,
    y_ss, y_rs, p_ss, p_rs, d_ss, d_rs,
):
    rows, features = x_enc.shape
    seq = rows // micro
    width = features // n
    heads = width // HEAD
    me = lax.axis_index("section")
    mine = pl.ds(pl.multiple_of(me * width, width), width)
    peers = [lax.rem(me + k, n) for k in range(1, n)]
    behind = [lax.rem(me + n - k, n) for k in range(1, n)]

    def cols(j):
        return slice(j * width, (j + 1) * width)

    barrier = pltpu.get_barrier_semaphore()
    for peer in peers:
        pl.semaphore_signal(
            barrier, inc=1, device_id={"section": peer}, device_id_type=pl.DeviceIdType.MESH
        )
    pl.semaphore_wait(barrier, n - 1)

    def push(src, dst, send, recv, peer):
        copy = pltpu.make_async_remote_copy(
            src_ref=src, dst_ref=dst, send_sem=send, recv_sem=recv,
            device_id={"section": peer}, device_id_type=pl.DeviceIdType.MESH,
        )
        copy.start()
        return copy

    pending = []

    def layer_in(layer, j):
        if layer == 0:
            return x_enc[:, cols(j)].astype(F32)
        if layer == 1:
            return x_one[j].astype(F32)
        return y_buf[layer - 1, j].astype(F32)

    def own_in(layer):
        if layer == 0:
            return x_enc[:, mine]
        if layer == 1:
            return x_one[me]
        return y_buf[layer - 1, me]

    def own_source(layer):
        return x_enc[:, mine] if layer == 0 else y_buf[0, me]

    inv_in = [None] * n
    inv_src = [None] * n

    def keys_of(layer, source):
        return (source.astype(F32) * inv_src[layer] * gain[layer : layer + 1, mine].astype(F32)).astype(BF16)

    for layer in range(n):
        if layer == 1:
            for j in range(n):
                x_one[j] = (x_dec[:, cols(j)].astype(F32) + y_buf[0, j].astype(F32)).astype(BF16)
            inv_memory = inv_norm([y_buf[0, j].astype(F32) for j in range(n)], features)
        inv = inv_norm([layer_in(layer, j) for j in range(n)], features)
        inv_in[layer] = inv
        inv_src[layer] = inv if layer == 0 else inv_memory
        query = jnp.zeros((rows, width), F32)
        for j in range(n):
            part = (layer_in(layer, j) * inv * gain[layer : layer + 1, cols(j)].astype(F32)).astype(BF16)
            nq_ref[layer, :, cols(j)] = part
            query = query + dot(part, weights[layer, cols(j), :], 1, 0)
        query = query.astype(BF16)
        q_buf[layer] = query
        source = own_source(layer)
        keys = keys_of(layer, source)
        bands = []
        for m in range(micro):
            r = slice(m * seq, (m + 1) * seq)
            pieces = []
            for h in range(heads):
                c = slice(h * HEAD, (h + 1) * HEAD)
                probs = softmax_parts(query[r, c], keys[r, c]).astype(BF16)
                pieces.append(dot(probs, source[r, c], 1, 0))
            bands.append(jnp.concatenate(pieces, axis=1))
        mixed = jnp.concatenate(bands, axis=0).astype(BF16).astype(F32)
        y_buf[layer, me] = (own_in(layer).astype(F32) + mix_scale * mixed).astype(BF16)
        copies = [
            push(y_buf.at[layer, me], y_buf.at[layer, me], y_ss.at[layer, k], y_rs.at[layer, k], peer)
            for k, peer in enumerate(peers)
        ]
        for copy in copies:
            copy.wait_recv()
        pending += copies

    for j in range(n):
        out_ref[:, cols(j)] = y_buf[me, j]

    d_result = d_last[:, mine]
    d_memory = jnp.zeros((rows, width), F32)
    for layer in range(n - 1, -1, -1):
        g = gain[layer : layer + 1, mine].astype(F32)
        source = own_source(layer)
        keys = keys_of(layer, source)
        query = q_buf[layer]
        d_mixed = (mix_scale * d_result.astype(F32)).astype(BF16)
        dq_bands, dk_bands, dv_bands = [], [], []
        for m in range(micro):
            r = slice(m * seq, (m + 1) * seq)
            dq_p, dk_p, dv_p = [], [], []
            for h in range(heads):
                c = slice(h * HEAD, (h + 1) * HEAD)
                probs = softmax_parts(query[r, c], keys[r, c])
                d_probs = dot(d_mixed[r, c], source[r, c], 1, 1).astype(BF16).astype(F32)
                dv_p.append(dot(probs.astype(BF16), d_mixed[r, c], 0, 0))
                inner = jnp.sum(d_probs * probs, axis=-1, keepdims=True)
                d_scores = (probs * (d_probs - inner) * HEAD ** (-0.5)).astype(BF16)
                dq_p.append(dot(d_scores, keys[r, c], 1, 0))
                dk_p.append(dot(d_scores, query[r, c], 0, 0))
            dq_bands.append(jnp.concatenate(dq_p, axis=1))
            dk_bands.append(jnp.concatenate(dk_p, axis=1))
            dv_bands.append(jnp.concatenate(dv_p, axis=1))
        d_query = jnp.concatenate(dq_bands, axis=0).astype(BF16)
        d_keys = jnp.concatenate(dk_bands, axis=0).astype(BF16).astype(F32)
        d_values = jnp.concatenate(dv_bands, axis=0).astype(BF16).astype(F32)
        dq_ref[layer] = d_query
        q_sum = jnp.sum(d_query.astype(F32) * query.astype(F32), axis=-1, keepdims=True)
        k_sum = jnp.sum(d_keys * keys.astype(F32), axis=-1, keepdims=True)
        q_hi = q_sum.astype(BF16).astype(F32)
        k_hi = k_sum.astype(BF16).astype(F32)
        lane = lax.broadcasted_iota(jnp.int32, (rows, TAIL), 1)
        tail = jnp.where(
            lane == 0, q_hi, jnp.where(lane == 1, q_sum - q_hi, jnp.where(lane == 2, k_hi, k_sum - k_hi))
        ).astype(BF16)
        for j in range(n):
            p_send[layer, j, :, :width] = dot(d_query, weights[layer, cols(j), :], 1, 1).astype(BF16)
            p_send[layer, j, :, width:] = tail
        copies = [
            push(p_send.at[layer, peer], p_recv.at[layer, me], p_ss.at[layer, k], p_rs.at[layer, k], peer)
            for k, peer in enumerate(peers)
        ]
        for copy in copies:
            copy.wait_recv()
        pending += copies
        blocks = [p_send[layer, me]] + [p_recv[layer, b] for b in behind]
        d_normed = sum(b[:, :width].astype(F32) for b in blocks).astype(BF16).astype(F32)
        sums = sum(b[:, width:].astype(F32) for b in blocks)
        q_tot = sums[:, 0:1] + sums[:, 1:2]
        k_tot = sums[:, 2:3] + sums[:, 3:4]
        inv, inv_m = inv_in[layer], inv_src[layer]
        x_own = own_in(layer).astype(F32)
        s_own = source.astype(F32)
        d_input = d_result.astype(F32) + inv * (g * d_normed) - x_own * (inv * inv * q_tot * (1.0 / features))
        d_source = inv_m * (g * d_keys) - s_own * (inv_m * inv_m * k_tot * (1.0 / features)) + d_values
        dg_ref[layer : layer + 1, :] = jnp.sum(
            x_own * inv * d_normed + s_own * inv_m * d_keys, axis=0, keepdims=True
        )
        if layer == 0:
            d_own[0] = (d_input + d_source).astype(BF16)
        else:
            d_result = d_input.astype(BF16)
            d_own[layer] = d_result
            d_memory = d_memory + d_source
            if layer == 1:
                d_result = (d_memory + d_result.astype(F32)).astype(BF16)

    copies = [
        push(d_own.at[peer], d_recv.at[me], d_ss.at[k], d_rs.at[k], peer) for k, peer in enumerate(peers)
    ]
    d_recv[me] = d_own[me]
    for copy in copies:
        copy.wait_recv()
    for j in range(n):
        din_ref[:, cols(j)] = d_recv[j]
    for copy in pending + copies:
        copy.wait_send()


def cascade(n, micro, x_enc, x_dec, d_last, weights, gain):
    rows, features = x_enc.shape
    width = features // n
    vmem = pl.BlockSpec(memory_space=pltpu.VMEM)
    sds = jax.ShapeDtypeStruct
    dma = pltpu.SemaphoreType.DMA
    return pl.pallas_call(
        functools.partial(cascade_kernel, n, micro),
        out_shape=(
            sds((rows, features), BF16),
            sds((rows, features), BF16),
            sds((n, rows, features), BF16),
            sds((n, rows, width), BF16),
            sds((n, width), F32),
        ),
        in_specs=[vmem] * 5,
        out_specs=[vmem] * 5,
        scratch_shapes=[
            pltpu.VMEM((n, n, rows, width), BF16),
            pltpu.VMEM((n, rows, width), BF16),
            pltpu.VMEM((n, n, rows, width + TAIL), BF16),
            pltpu.VMEM((n, n, rows, width + TAIL), BF16),
            pltpu.VMEM((n, rows, width), BF16),
            pltpu.VMEM((n, rows, width), BF16),
            pltpu.VMEM((n, rows, width), BF16),
            dma((n, n - 1)), dma((n, n - 1)),
            dma((n, n - 1)), dma((n, n - 1)),
            dma((n - 1,)), dma((n - 1,)),
        ],
        compiler_params=pltpu.CompilerParams(
            collective_id=0, has_side_effects=True, vmem_limit_bytes=56 * 1024 * 1024
        ),
    )(x_enc, x_dec, d_last, weights, gain)


def shards(x_enc, x_dec, d_out, lengths, w_query, gain):
    n = lax.axis_size("section")
    micro, seq, features = x_enc.shape
    rows = micro * seq
    width = features // n
    row_index = lax.broadcasted_iota(jnp.int32, (micro, seq, 1), 1)
    d_last = jnp.where(row_index < lengths[:, :, None], d_out, jnp.zeros_like(d_out))
    split = w_query[0].reshape(-1, n, width).transpose(1, 0, 2)
    own = lax.all_to_all(split, "section", 0, 0, tiled=True)
    weights = lax.all_gather(own, "dp", axis=1, tiled=True)
    full_gain = lax.all_gather(lax.all_gather(gain, "dp", axis=1, tiled=True), "section", axis=0, tiled=True)
    out, d_in, normed, d_query, d_gain = cascade(
        n, micro, x_enc.reshape(rows, features), x_dec.reshape(rows, features),
        d_last.reshape(rows, features), weights, full_gain,
    )
    part = jnp.einsum("lrf,lrc->lfc", normed, d_query, preferred_element_type=F32).astype(BF16)
    part = lax.psum_scatter(part, "dp", scatter_dimension=1, tiled=True)
    grad = lax.all_to_all(part, "section", 0, 0, tiled=True)
    grad = grad.transpose(1, 0, 2).reshape(1, -1, features).astype(F32)
    gains = lax.psum_scatter(
        lax.all_to_all(d_gain.astype(BF16), "section", 0, 0, tiled=True).reshape(1, features),
        "dp", scatter_dimension=1, tiled=True,
    ).astype(F32)
    return (
        out.reshape(1, micro, seq, features),
        d_in.reshape(1, micro, seq, features),
        grad,
        gains,
    )


def solution(mesh):
    in_specs = (
        P(None, "dp", None), P(None, "dp", None), P(None, "dp", None),
        P(None, "dp"), P("section", "dp", None), P("section", "dp"),
    )
    out_specs = (
        P("section", None, "dp", None), P("section", None, "dp", None),
        P("section", "dp", None), P("section", "dp"),
    )
    return jax.shard_map(shards, mesh=mesh, in_specs=in_specs, out_specs=out_specs, check_vma=False)
```

time: 700 us -> 476 us (0.68); the launches traced: 690 us -> 476 us
  waiting for transfers between devices: 489 us -> 303 us
  Pallas kernels: 0 us -> 80.3 us
  other arithmetic: 58.9 us -> 2.5 us
  matrix products: 43.3 us -> 7.27 us
  blocking collectives: 22.6 us -> 53 us
  starting transfers between devices: 24.3 us -> 3.64 us
  local copies, waits for them, and re-layouts: 25.9 us -> 12.3 us
  loops' own time: 10.6 us -> 0 us
    ppermute x8 -> x0, waiting for transfers between devices: 99.1 us -> none  [from_behind(): return lax.ppermute(block, axis, route)]
    psum x3 -> x0, waiting for transfers between devices: 93.8 us -> none  [the longest x2 58 us: from_root(): return lax.psum(kept, axis)]
    pallas_call x0 -> x1, Pallas kernels: none -> 80.3 us  [cascade(): pl.pallas_call(functools.partial(cascade_kernel, n, micro), out_shape=(sd...]
    dot_general x21 -> x1, matrix products: 43.3 us -> 7.27 us  [shards(): jnp.einsum('lrf,lrc->lfc', normed, d_query, preferred_element_type=F32)]
    select_n x26 -> x0, other arithmetic: 35.3 us -> none  [the longest x4 8.85 us: shards(): jnp.where(active, normed_buf.at[slot_index].set(parts[3]), normed_buf)]
    all_to_all x0 -> x2, blocking collectives: none -> 26.4 us  [the longest x1 18.7 us: shards(): own = lax.all_to_all(split, 'section', 0, 0, tiled=True)]
    ppermute x8 -> x0, starting transfers between devices: 23.8 us -> none  [from_behind(): return lax.ppermute(block, axis, route)]
    unnamed x7 -> x4, waiting for transfers between devices: 43.3 us -> 65.5 us
  transfers between devices with their start and end apart: 14 -> 4, of which waited for: 13 -> 3; matrix products, arithmetic and copies ran while one was open for 7% -> 1% of each run, Pallas kernels for 0% -> 0%
where the time goes in v1:
time: 476 us
  waiting for transfers between devices  303 us (64%)
  Pallas kernels  80.3 us (17%)
  blocking collectives  53 us (11%)
  between operations  13.8 us (3%)
  local copies, waits for them, and re-layouts  12.3 us (3%)
  matrix products  7.27 us (2%)
    reduce_scatter x1, waiting for transfers between devices, shards(): part = lax.psum_scatter(part, 'dp', scatter_dimension=1, tiled=True)  140 us
    all_gather x1, waiting for transfers between devices, shards(): weights = lax.all_gather(own, 'dp', axis=1, tiled=True)  97.7 us
    pallas_call x1, Pallas kernels, cascade(): pl.pallas_call(functools.partial(cascade_kernel, n, micro), out_shape=(sd...  80.3 us
    unnamed x4, waiting for transfers between devices  65.5 us
    all_gather x1, blocking collectives, shards(): lax.all_gather(gain, 'dp', axis=1, tiled=True)  21.4 us
    all_to_all x1, blocking collectives, shards(): own = lax.all_to_all(split, 'section', 0, 0, tiled=True)  18.7 us
  transfers between devices with their start and end apart: 4, of which 3 were waited for; matrix products, arithmetic and copies ran while one was open for 1% of the time, Pallas kernels for 0%

profile of v1, /device:TPU:0, one launch (start us, length us, event | category | flops | bytes accessed | tf_op | source)
XLA Modules:
  0.0 475.6 jit_solution(15941129736678353725)
XLA Ops:
  7.2 0.0 all-gather.3.cloned.1.call-start
  7.2 1.5 copy.22
  8.7 0.5 copy.23
  9.3 18.7 %all_to_all.19 = bf16[4,256,512]{2,1,0:T(8,128)(2,1)} all-to-all(bf16[4,256,512]{2,1,0:T(8,128)(2,1)S(1)} %bitcast.23), channel_id=1, replica_groups=mesh['section'=4,'dp'=8] {'section'}, dimensions={0} | all-to-all | bytes 2097152 | tf_op jit(solution)/shard_map/all_to_all | solution.py:253
  28.0 0.0 all-gather.3.cloned.1.call-update
  28.0 0.0 reduce-scatter.5.cloned.1.call-start
  28.1 21.4 %all_gather.10 = bf16[1,2048]{1,0:T(2,128)(2,1)S(1)} all-gather(bf16[1,256]{1,0:T(2,128)(2,1)S(1)} %copy-done.4), channel_id=1, replica_groups=mesh['section'=4,'dp'=8] {'dp'}, dimensions={1}, use_global_device_ids=true | all-gather | bytes 4608 | tf_op jit(solution)/shard_map/all_gather | solution.py:255
  49.5 5.2 %all-gather = bf16[4,1,2048]{2,1,0:T(2,128)(2,1)S(1)} all-gather(bf16[1,1,2048]{2,1,0:T(2,128)(2,1)S(1)} %bitcast.34), channel_id=1, replica_groups=mesh['section'=4,'dp'=8] {'section'}, dimensions={0}, use_global_device_ids=true | all-gather | bytes 20480 | tf_op jit(solution)/shard_map/all_gather | solution.py:255
  54.7 0.6 copy.33
  55.3 0.1 iota_compare_fusion
  55.3 0.9 broadcast_select_fusion
  56.2 97.7 %all-gather.3.cloned.1.call-done.weights = bf16[4,2048,512]{2,1,0:T(8,128)(2,1)} async-done(((bf16[4,256,512]{2,1,0:T(8,128)(2,1)}), bf16[4,2048,512]{2,1,0:T(8,128)(2,1)}) %all-gather.3.cloned.1.call-update) | async-done | bytes 8388624 | tf_op jit(solution)/shard_map/all_gather | solution.py:254
  153.9 80.3 %shard_map.96 = (bf16[128,2048]{1,0:T(8,128)(2,1)}, bf16[128,2048]{1,0:T(8,128)(2,1)}, bf16[4,128,2048]{2,1,0:T(8,128)(2,1)}, bf16[4,128,512]{2,1,0:T(8,128)(2,1)}, f32[4,512]{1,0:T(4,128)}) custom-call(bf16[128,2048]{1,0:T(8,128)(2,1)} %bitcast.27, bf16[128,2048]{1,0:T(8,128)(2,1)} %bitcast.28, bf16[128,2048]{1,0:T(8,128)(2,1)} %bitcast.25, ...), custom_call_target="tpu_custom_call" | custom-call | tf_op jit(solution)/shard_map/pallas_call | solution.py:216
  234.2 7.3 %convolution_convert_fusion = bf16[4,2048,512]{2,1,0:T(8,128)(2,1)} fusion(bf16[4,128,2048]{2,1,0:T(8,128)(2,1)} %get-tuple-element.11, bf16[4,128,512]{2,1,0:T(8,128)(2,1)} %get-tuple-element.12), kind=kOutput, calls=%fused_computation | convolution fusion | flops 1077936128 | bytes 11010048 | tf_op jit(solution)/shard_map/lrf,lrc->lfc/dot_general | solution.py:260
  241.5 0.0 reduce-scatter.5.cloned.1.call-update
  241.5 0.7 copy-done.3
  242.2 0.5 broadcast.14
  242.7 0.7 reduce
  243.4 7.7 %all_to_all.20 = bf16[4,2,256]{2,1,0:T(2,128)(2,1)S(1)} all-to-all(bf16[4,2,256]{2,1,0:T(2,128)(2,1)S(1)} %reshape.79), channel_id=1, replica_groups=mesh['section'=4,'dp'=8] {'section'}, dimensions={0} | all-to-all | bytes 8192 | tf_op jit(solution)/shard_map/all_to_all | solution.py:265
  251.1 139.6 %reduce-scatter.5.cloned.1.call-done = bf16[4,256,512]{2,1,0:T(8,128)(2,1)} async-done(((bf16[4,2048,512]{2,1,0:T(8,128)(2,1)}), bf16[4,256,512]{2,1,0:T(8,128)(2,1)}) %reduce-scatter.5.cloned.1.call-update) | async-done | bytes 1048592 | tf_op jit(solution)/shard_map/reduce_scatter | solution.py:261
  390.7 3.5 all-to-all-start.1
  394.2 0.0 reduce-scatter.7.cloned.1.call-start
  394.3 1.1 copy.29
  395.3 0.0 reduce-scatter.7.cloned.1.call-update
  395.4 65.4 %reduce-scatter.7.cloned.1.call-done = bf16[256,1]{1,0:T(8,128)(2,1)} async-done(((bf16[2048,1]{1,0:T(8,128)(2,1)}), bf16[256,1]{1,0:T(8,128)(2,1)}) %reduce-scatter.7.cloned.1.call-update) | async-done | bytes 528
  460.8 0.9 copy.30
  461.7 0.6 convert_element_type.31
  462.3 0.3 convert_bitcast_fusion
  462.6 1.9 copy.25
  464.5 3.0 copy.27
  467.4 0.8 copy.37
  468.2 0.8 copy.38
  (15 shorter events, 0.1 us)
Async XLA Ops:
  7.2 146.8 %all-gather.3.cloned.1.call-start = ((), (), s32[]{:S(2)}) async-start(), calls=%async_computation.5 | async-start | bytes 9437184 | tf_op jit(solution)/shard_map/all_gather | solution.py:254
  9.2 18.8 %copy-start.4 = (bf16[1,256]{1,0:T(2,128)(2,1)S(1)}, bf16[1,256]{1,0:T(2,128)(2,1)}, u32[]{:S(2)}) copy-start(bf16[1,256]{1,0:T(2,128)(2,1)} %param.11) | copy-start | bytes 1540
  9.3 46.0 %copy-start.5 = (s32[2,1]{0,1:T(1,128)S(1)}, s32[2,1]{0,1:T(1,128)}, u32[]{:S(2)}) copy-start(s32[2,1]{0,1:T(1,128)} %param.9) | copy-start | bytes 28
  9.3 46.1 %copy-start.2 = (bf16[2,64,2048]{2,1,0:T(8,128)(2,1)S(1)}, bf16[2,64,2048]{2,1,0:T(8,128)(2,1)}, u32[]{:S(2)}) copy-start(bf16[2,64,2048]{2,1,0:T(8,128)(2,1)} %param.8) | copy-start | bytes 1572868
  28.0 362.7 %reduce-scatter.5.cloned.1.call-start = ((), (), s32[]{:S(2)}) async-start(), calls=%async_computation.6 | async-start | bytes 9437184 | tf_op jit(solution)/shard_map/reduce_scatter | solution.py:261
  241.5 0.7 copy-start.3
  390.7 71.6 %all-to-all-start.1 = ((bf16[4,256,512]{2,1,0:T(8,128)(2,1)}), bf16[4,256,512]{2,1,0:T(8,128)(2,1)S(1)}, u32[]{:S(2)}, u32[]{:S(2)}) async-start(bf16[4,256,512]{2,1,0:T(8,128)(2,1)} %reduce-scatter.5.cloned.1.call-done), calls=%async_computation.2 | async-start | bytes 2097152 | tf_op jit(solution)/shard_map/all_to_all | solution.py:262
  394.2 66.6 %reduce-scatter.7.cloned.1.call-start = ((), (), s32[]{:S(2)}) async-start(), calls=%async_computation.7 | async-start | bytes 589824
  464.5 3.0 copy-start.1
  464.5 3.8 copy-start
Sparse Core Ops, SparseCore 0:
  28.1 125.7 all-gather.2
  241.7 148.9 reduce-scatter.4
  399.3 61.4 reduce-scatter.6

commit v2 on v1

--- a/solution.py
+++ b/solution.py
@@ -30,40 +30,164 @@
     return weights / jnp.sum(weights, axis=-1, keepdims=True)
 
 
+MESH = pl.DeviceIdType.MESH
+PAD = 16
+
+
+class Spread:
+    def __init__(self, buf, count, sems):
+        self.buf, self.count = buf, count
+        self.chain_s, self.chain_r, self.pair_s, self.pair_r = sems
+        here = lax.axis_index("dp")
+        self.place, self.side = here // 2, lax.rem(here, 2)
+
+    def copy(self, layer, place, side, send, recv, to_place, to_side):
+        block = self.buf.at[layer, place * 2 + side]
+        return pltpu.make_async_remote_copy(
+            src_ref=block, dst_ref=block, send_sem=send, recv_sem=recv,
+            device_id={"dp": to_place * 2 + to_side}, device_id_type=MESH,
+        )
+
+    def chain(self, layer, step, way):
+        sign = 1 if way == 0 else -1
+        return self.copy(
+            layer, self.place - sign * step, self.side,
+            self.chain_s.at[way, layer, step], self.chain_r.at[way, layer, step],
+            self.place + sign, self.side,
+        )
+
+    def pair(self, layer, step, way, side):
+        sign = 1 if way == 0 else -1
+        slot = step if way == 0 else self.count - 1 + step
+        return self.copy(
+            layer, self.place - sign * step, side,
+            self.pair_s.at[layer, slot], self.pair_r.at[layer, slot], self.place, 1 - self.side,
+        )
+
+    def holds(self, step, way):
+        return self.place >= step if way == 0 else self.place + step < self.count
+
+    def passes(self, step, way):
+        end = self.place + 1 < self.count if way == 0 else self.place >= 1
+        return jnp.logical_and(self.holds(step, way), end)
+
+    def arrived(self, layer, step, way):
+        sign = 1 if way == 0 else -1
+        return self.copy(
+            layer, self.place - sign * step, self.side,
+            self.chain_s.at[way, layer, step - 1], self.chain_r.at[way, layer, step - 1],
+            self.place + sign, self.side,
+        )
+
+    def pump(self, layer, step):
+        for way in (0, 1):
+            if step > 0:
+                @pl.when(self.holds(step, way))
+                def _():
+                    self.arrived(layer, step, way).wait_recv()
+
+            if step < self.count - 1:
+                @pl.when(self.passes(step, way))
+                def _():
+                    self.chain(layer, step, way).start()
+
+            if step == 0:
+                if way == 0:
+                    self.pair(layer, 0, 0, self.side).start()
+            else:
+                @pl.when(self.holds(step, way))
+                def _():
+                    self.pair(layer, step, way, self.side).start()
+
+    def finish(self, layer):
+        self.pair(layer, 0, 0, 1 - self.side).wait_recv()
+        for step in range(1, self.count):
+            for way in (0, 1):
+                @pl.when(self.holds(step, way))
+                def _():
+                    self.pair(layer, step, way, 1 - self.side).wait_recv()
+
+    def drain(self, layer):
+        self.pair(layer, 0, 0, self.side).wait_send()
+        for step in range(self.count):
+            for way in (0, 1):
+                if step < self.count - 1:
+                    @pl.when(self.passes(step, way))
+                    def _():
+                        self.chain(layer, step, way).wait_send()
+
+                if step > 0:
+                    @pl.when(self.holds(step, way))
+                    def _():
+                        self.pair(layer, step, way, self.side).wait_send()
+
+
 def cascade_kernel(
-    n, micro, x_enc, x_dec, d_last, weights, gain,
-    out_ref, din_ref, nq_ref, dq_ref, dg_ref,
-    y_buf, x_one, p_send, p_recv, d_own, d_recv, q_buf,
-    y_ss, y_rs, p_ss, p_rs, d_ss, d_rs,
+    n, nd, micro, x_enc, x_dec, d_last, payload,
+    out_ref, din_ref, grad_ref, dg_ref,
+    weights, dq_all, nq_own, nq_all, gain, y_buf, x_one, p_send, p_recv, d_own, d_recv, q_buf, g_send, g_recv,
+    y_ss, y_rs, p_ss, p_rs, d_ss, d_rs, g_ss, g_rs, a_ss, a_rs, n_ss, n_rs,
+    wz_s, wz_r, wy_s, wy_r, qz_s, qz_r, qy_s, qy_r,
 ):
     rows, features = x_enc.shape
     seq = rows // micro
     width = features // n
+    depth = features // nd
+    share = width // depth
+    half = nd // 2
     heads = width // HEAD
     me = lax.axis_index("section")
+    here = lax.axis_index("dp")
     mine = pl.ds(pl.multiple_of(me * width, width), width)
     peers = [lax.rem(me + k, n) for k in range(1, n)]
     behind = [lax.rem(me + n - k, n) for k in range(1, n)]
+    dp_peers = [lax.rem(here + k, nd) for k in range(1, nd)]
 
     def cols(j):
         return slice(j * width, (j + 1) * width)
 
     barrier = pltpu.get_barrier_semaphore()
     for peer in peers:
-        pl.semaphore_signal(
-            barrier, inc=1, device_id={"section": peer}, device_id_type=pl.DeviceIdType.MESH
-        )
-    pl.semaphore_wait(barrier, n - 1)
-
-    def push(src, dst, send, recv, peer):
-        copy = pltpu.make_async_remote_copy(
+        pl.semaphore_signal(barrier, inc=1, device_id={"section": peer}, device_id_type=MESH)
+    for peer in dp_peers:
+        pl.semaphore_signal(barrier, inc=1, device_id={"dp": peer}, device_id_type=MESH)
+    pl.semaphore_wait(barrier, n - 1 + nd - 1)
+
+    def describe(src, dst, send, recv, peer, axis="section"):
+        return pltpu.make_async_remote_copy(
             src_ref=src, dst_ref=dst, send_sem=send, recv_sem=recv,
-            device_id={"section": peer}, device_id_type=pl.DeviceIdType.MESH,
-        )
+            device_id={axis: peer}, device_id_type=MESH,
+        )
+
+    def push(*args):
+        copy = describe(*args)
         copy.start()
         return copy
 
     pending = []
+    w_spread = Spread(weights, half, (wz_s, wz_r, wy_s, wy_r))
+    q_spread = Spread(dq_all, half, (qz_s, qz_r, qy_s, qy_r))
+
+    for k, peer in enumerate(peers):
+        pending.append(
+            push(payload.at[peer], weights.at[me, here], a_ss.at[k], a_rs.at[me], peer)
+        )
+    weights[me, here] = payload[me]
+
+    def pump_weights(layer, step):
+        if step == 0:
+            @pl.when(me != layer)
+            def _():
+                describe(
+                    payload.at[me], weights.at[layer, here], a_ss.at[0], a_rs.at[layer], peers[0]
+                ).wait_recv()
+
+        w_spread.pump(layer, step)
+
+    def weight_clock(clock):
+        for layer in range(n):
+            if 0 <= clock - layer < half:
+                pump_weights(layer, clock - layer)
 
     def layer_in(layer, j):
         if layer == 0:
@@ -85,8 +209,14 @@
     inv_in = [None] * n
     inv_src = [None] * n
 
+    def gain_of(layer):
+        return gain[layer, me][0:1].astype(F32)
+
     def keys_of(layer, source):
-        return (source.astype(F32) * inv_src[layer] * gain[layer : layer + 1, mine].astype(F32)).astype(BF16)
+        return (source.astype(F32) * inv_src[layer] * gain_of(layer)).astype(BF16)
+
+    for clock in range(half):
+        weight_clock(clock)
 
     for layer in range(n):
         if layer == 1:
@@ -96,11 +226,19 @@
         inv = inv_norm([layer_in(layer, j) for j in range(n)], features)
         inv_in[layer] = inv
         inv_src[layer] = inv if layer == 0 else inv_memory
+        weight_clock(half + layer)
+        w_spread.finish(layer)
         query = jnp.zeros((rows, width), F32)
         for j in range(n):
-            part = (layer_in(layer, j) * inv * gain[layer : layer + 1, cols(j)].astype(F32)).astype(BF16)
-            nq_ref[layer, :, cols(j)] = part
-            query = query + dot(part, weights[layer, cols(j), :], 1, 0)
+            scaled = layer_in(layer, j) * inv
+            for i in range(share):
+                b = j * share + i
+                lanes = slice(i * depth, (i + 1) * depth)
+                row = weights[layer, b, depth : depth + PAD, :depth]
+                gain[layer, j, :, lanes] = row
+                part = (scaled[:, lanes] * row[0:1].astype(F32)).astype(BF16)
+                nq_own[layer, b] = part
+                query = query + dot(part, weights[layer, b, :depth, :], 1, 0)
         query = query.astype(BF16)
         q_buf[layer] = query
         source = own_source(layer)
@@ -120,17 +258,61 @@
             push(y_buf.at[layer, me], y_buf.at[layer, me], y_ss.at[layer, k], y_rs.at[layer, k], peer)
             for k, peer in enumerate(peers)
         ]
-        for copy in copies:
+        if layer < n - 1:
+            for copy in copies:
+                copy.wait_recv()
+        else:
+            last = copies
+        pending += copies
+
+    nq_copies = []
+    for layer in range(n - 1, -1, -1):
+        for k, peer in enumerate(dp_peers):
+            nq_copies.append(
+                push(
+                    nq_own.at[layer, peer], nq_all.at[layer, here],
+                    n_ss.at[layer, k], n_rs.at[layer, k], peer, "dp",
+                )
+            )
+        nq_all[layer, here] = nq_own[layer, here]
+
+    def query_clock(clock):
+        for i in range(n):
+            if 0 <= clock - i < half:
+                q_spread.pump(n - 1 - i, clock - i)
+
+    def gradient(layer):
+        q_spread.finish(layer)
+        i = n - 1 - layer
+        for copy in nq_copies[i * (nd - 1) : (i + 1) * (nd - 1)]:
             copy.wait_recv()
-        pending += copies
-
-    for j in range(n):
-        out_ref[:, cols(j)] = y_buf[me, j]
+        left = nq_all[layer].reshape(nd * rows, depth)
+        right = jnp.concatenate([dq_all[layer, b, :rows, :] for b in range(nd)], axis=0)
+        g_send[layer, :depth, :] = dot(left, right, 0, 0).astype(BF16)
+        total = sum(dq_all[layer, b, rows : rows + PAD, :].astype(F32) for b in range(nd))
+        g_send[layer, depth:, :] = total.astype(BF16)
+        deliver(g_send, g_recv, g_ss, g_rs, layer)
+
+    def to_layer(buf, landing, send, recv, layer):
+        return describe(buf.at[layer], landing.at[me], send.at[layer], recv.at[me], layer)
+
+    def deliver(buf, landing, send, recv, layer):
+        @pl.when(me != layer)
+        def _():
+            to_layer(buf, landing, send, recv, layer).start()
+
+        @pl.when(me == layer)
+        def _():
+            landing[me] = buf[layer]
+
+    def collect(buf, landing, send, recv):
+        for b in behind:
+            describe(buf.at[0], landing.at[b], send.at[0], recv.at[b], b).wait_recv()
 
     d_result = d_last[:, mine]
     d_memory = jnp.zeros((rows, width), F32)
     for layer in range(n - 1, -1, -1):
-        g = gain[layer : layer + 1, mine].astype(F32)
+        g = gain_of(layer)
         source = own_source(layer)
         keys = keys_of(layer, source)
         query = q_buf[layer]
@@ -154,7 +336,6 @@
         d_query = jnp.concatenate(dq_bands, axis=0).astype(BF16)
         d_keys = jnp.concatenate(dk_bands, axis=0).astype(BF16).astype(F32)
         d_values = jnp.concatenate(dv_bands, axis=0).astype(BF16).astype(F32)
-        dq_ref[layer] = d_query
         q_sum = jnp.sum(d_query.astype(F32) * query.astype(F32), axis=-1, keepdims=True)
         k_sum = jnp.sum(d_keys * keys.astype(F32), axis=-1, keepdims=True)
         q_hi = q_sum.astype(BF16).astype(F32)
@@ -163,8 +344,12 @@
         tail = jnp.where(
             lane == 0, q_hi, jnp.where(lane == 1, q_sum - q_hi, jnp.where(lane == 2, k_hi, k_sum - k_hi))
         ).astype(BF16)
+        for b in range(nd):
+            lanes = slice((b % share) * depth, (b % share + 1) * depth)
+            p_send[layer, b // share, :, lanes] = dot(
+                d_query, weights[layer, b, :depth, :], 1, 1
+            ).astype(BF16)
         for j in range(n):
-            p_send[layer, j, :, :width] = dot(d_query, weights[layer, cols(j), :], 1, 1).astype(BF16)
             p_send[layer, j, :, width:] = tail
         copies = [
             push(p_send.at[layer, peer], p_recv.at[layer, me], p_ss.at[layer, k], p_rs.at[layer, k], peer)
@@ -183,9 +368,10 @@
         s_own = source.astype(F32)
         d_input = d_result.astype(F32) + inv * (g * d_normed) - x_own * (inv * inv * q_tot * (1.0 / features))
         d_source = inv_m * (g * d_keys) - s_own * (inv_m * inv_m * k_tot * (1.0 / features)) + d_values
-        dg_ref[layer : layer + 1, :] = jnp.sum(
-            x_own * inv * d_normed + s_own * inv_m * d_keys, axis=0, keepdims=True
-        )
+        gain_part = jnp.sum(x_own * inv * d_normed + s_own * inv_m * d_keys, axis=0, keepdims=True)
+        dq_all[layer, here, :rows, :] = d_query
+        dq_all[layer, here, rows:, :] = jnp.broadcast_to(gain_part, (PAD, width)).astype(BF16)
+        query_clock(n - 1 - layer)
         if layer == 0:
             d_own[0] = (d_input + d_source).astype(BF16)
         else:
@@ -194,37 +380,60 @@
             d_memory = d_memory + d_source
             if layer == 1:
                 d_result = (d_memory + d_result.astype(F32)).astype(BF16)
-
-    copies = [
-        push(d_own.at[peer], d_recv.at[me], d_ss.at[k], d_rs.at[k], peer) for k, peer in enumerate(peers)
-    ]
-    d_recv[me] = d_own[me]
-    for copy in copies:
+        deliver(d_own, d_recv, d_ss, d_rs, layer)
+
+    for copy in last:
         copy.wait_recv()
     for j in range(n):
-        din_ref[:, cols(j)] = d_recv[j]
-    for copy in pending + copies:
+        out_ref[:, cols(j)] = y_buf[me, j]
+    done = 0
+    for clock in range(n, n + half):
+        query_clock(clock)
+        while done < n and done + half - 1 <= clock:
+            if done == n - 1:
+                collect(d_own, d_recv, d_ss, d_rs)
+                for j in range(n):
+                    din_ref[:, cols(j)] = d_recv[j]
+            gradient(n - 1 - done)
+            done += 1
+    collect(g_send, g_recv, g_ss, g_rs)
+    for j in range(n):
+        grad_ref[:, cols(j)] = g_recv[j, :depth, :].astype(F32)
+        dg_ref[:, cols(j)] = g_recv[j, depth : depth + PAD, :][0:1].astype(F32)
+    for copy in pending + nq_copies:
         copy.wait_send()
-
-
-def cascade(n, micro, x_enc, x_dec, d_last, weights, gain):
+    for layer in range(n):
+        w_spread.drain(layer)
+        q_spread.drain(layer)
+
+        @pl.when(me != layer)
+        def _():
+            to_layer(d_own, d_recv, d_ss, d_rs, layer).wait_send()
+            to_layer(g_send, g_recv, g_ss, g_rs, layer).wait_send()
+
+
+def cascade(n, nd, micro, x_enc, x_dec, d_last, payload):
     rows, features = x_enc.shape
-    width = features // n
+    width, depth, half = features // n, features // nd, nd // 2
     vmem = pl.BlockSpec(memory_space=pltpu.VMEM)
     sds = jax.ShapeDtypeStruct
     dma = pltpu.SemaphoreType.DMA
     return pl.pallas_call(
-        functools.partial(cascade_kernel, n, micro),
+        functools.partial(cascade_kernel, n, nd, micro),
         out_shape=(
             sds((rows, features), BF16),
             sds((rows, features), BF16),
-            sds((n, rows, features), BF16),
-            sds((n, rows, width), BF16),
-            sds((n, width), F32),
+            sds((depth, features), F32),
+            sds((1, features), F32),
         ),
-        in_specs=[vmem] * 5,
-        out_specs=[vmem] * 5,
+        in_specs=[vmem] * 4,
+        out_specs=[vmem] * 4,
         scratch_shapes=[
+            pltpu.VMEM((n, nd, depth + PAD, width), BF16),
+            pltpu.VMEM((n, nd, rows + PAD, width), BF16),
+            pltpu.VMEM((n, nd, rows, depth), BF16),
+            pltpu.VMEM((n, nd, rows, depth), BF16),
+            pltpu.VMEM((n, n, PAD, width), BF16),
             pltpu.VMEM((n, n, rows, width), BF16),
             pltpu.VMEM((n, rows, width), BF16),
             pltpu.VMEM((n, n, rows, width + TAIL), BF16),
@@ -232,43 +441,44 @@
             pltpu.VMEM((n, rows, width), BF16),
             pltpu.VMEM((n, rows, width), BF16),
             pltpu.VMEM((n, rows, width), BF16),
+            pltpu.VMEM((n, depth + PAD, width), BF16),
+            pltpu.VMEM((n, depth + PAD, width), BF16),
             dma((n, n - 1)), dma((n, n - 1)),
             dma((n, n - 1)), dma((n, n - 1)),
-            dma((n - 1,)), dma((n - 1,)),
-        ],
+            dma((n,)), dma((n,)),
+            dma((n,)), dma((n,)),
+            dma((n - 1,)), dma((n,)),
+            dma((n, nd - 1)), dma((n, nd - 1)),
+        ]
+        + [
+            dma((2, n, half)), dma((2, n, half)),
+            dma((n, 2 * half)), dma((n, 2 * half)),
+        ] * 2,
         compiler_params=pltpu.CompilerParams(
             collective_id=0, has_side_effects=True, vmem_limit_bytes=56 * 1024 * 1024
         ),
-    )(x_enc, x_dec, d_last, weights, gain)
+    )(x_enc, x_dec, d_last, payload)
 
 
 def shards(x_enc, x_dec, d_out, lengths, w_query, gain):
-    n = lax.axis_size("section")
+    n, nd = lax.axis_size("section"), lax.axis_size("dp")
     micro, seq, features = x_enc.shape
     rows = micro * seq
-    width = features // n
+    width, depth = features // n, features // nd
     row_index = lax.broadcasted_iota(jnp.int32, (micro, seq, 1), 1)
     d_last = jnp.where(row_index < lengths[:, :, None], d_out, jnp.zeros_like(d_out))
-    split = w_query[0].reshape(-1, n, width).transpose(1, 0, 2)
-    own = lax.all_to_all(split, "section", 0, 0, tiled=True)
-    weights = lax.all_gather(own, "dp", axis=1, tiled=True)
-    full_gain = lax.all_gather(lax.all_gather(gain, "dp", axis=1, tiled=True), "section", axis=0, tiled=True)
-    out, d_in, normed, d_query, d_gain = cascade(
-        n, micro, x_enc.reshape(rows, features), x_dec.reshape(rows, features),
-        d_last.reshape(rows, features), weights, full_gain,
+    split = w_query[0].reshape(depth, n, width).transpose(1, 0, 2)
+    gain_rows = jnp.broadcast_to(jnp.pad(gain[0], (0, width - depth)), (n, PAD, width))
+    payload = jnp.concatenate([split, gain_rows], axis=1)
+    out, d_in, grad, gains = cascade(
+        n, nd, micro, x_enc.reshape(rows, features), x_dec.reshape(rows, features),
+        d_last.reshape(rows, features), payload,
     )
-    part = jnp.einsum("lrf,lrc->lfc", normed, d_query, preferred_element_type=F32).astype(BF16)
-    part = lax.psum_scatter(part, "dp", scatter_dimension=1, tiled=True)
-    grad = lax.all_to_all(part, "section", 0, 0, tiled=True)
-    grad = grad.transpose(1, 0, 2).reshape(1, -1, features).astype(F32)
-    gains = lax.psum_scatter(
-        lax.all_to_all(d_gain.astype(BF16), "section", 0, 0, tiled=True).reshape(1, features),
-        "dp", scatter_dimension=1, tiled=True,
-    ).astype(F32)
+    gains = lax.dynamic_slice_in_dim(gains, lax.axis_index("dp") * depth, depth, axis=1)
     return (
         out.reshape(1, micro, seq, features),
         d_in.reshape(1, micro, seq, features),
-        grad,
+        grad[None],
         gains,
     )
 

time: 476 us -> 237 us (0.50)
  waiting for transfers between devices: 303 us -> 0 us
  Pallas kernels: 80.3 us -> 223 us
  blocking collectives: 53 us -> 0 us
  between operations: 13.8 us -> 0.67 us
  matrix products: 7.27 us -> 0 us
    pallas_call x1, Pallas kernels: 80.3 us -> 223 us  [cascade(): pl.pallas_call(functools.partial(cascade_kernel, n, nd, micro), out_shape...]
    reduce_scatter x1 -> x0, waiting for transfers between devices: 140 us -> none  [shards(): part = lax.psum_scatter(part, 'dp', scatter_dimension=1, tiled=True)]
    all_gather x1 -> x0, waiting for transfers between devices: 97.7 us -> none  [shards(): weights = lax.all_gather(own, 'dp', axis=1, tiled=True)]
    unnamed x4 -> x0, waiting for transfers between devices: 65.5 us -> none
    all_gather x2 -> x0, blocking collectives: 26.6 us -> none  [the longest x1 21.4 us: shards(): lax.all_gather(gain, 'dp', axis=1, tiled=True)]
    all_to_all x2 -> x0, blocking collectives: 26.4 us -> none  [the longest x1 18.7 us: shards(): own = lax.all_to_all(split, 'section', 0, 0, tiled=True)]
    dot_general x1 -> x0, matrix products: 7.27 us -> none  [shards(): jnp.einsum('lrf,lrc->lfc', normed, d_query, preferred_element_type=F32)]
  transfers between devices with their start and end apart: 4 -> 0, of which waited for: 3 -> 0; matrix products, arithmetic and copies ran while one was open for 1% -> 0% of each run, Pallas kernels for 0% -> 0%
where the time goes in v2:
time: 237 us
  Pallas kernels  223 us (94%)
  local copies, waits for them, and re-layouts  8.5 us (4%)
  other arithmetic  4.46 us (2%)
    pallas_call x1, Pallas kernels, cascade(): pl.pallas_call(functools.partial(cascade_kernel, n, nd, micro), out_shape...  223 us
    unnamed x6, local copies, waits for them, and re-layouts  6.56 us

profile of v2, /device:TPU:0, one launch (start us, length us, event | category | flops | bytes accessed | tf_op | source)
XLA Modules:
  0.0 236.7 jit_solution(9760376162675558972)
XLA Ops:
  0.6 0.7 iota_compare_fusion
  1.4 0.7 reduce
  2.1 1.9 broadcast_select_fusion
  4.0 1.5 copy.10
  5.5 0.5 copy.11
  6.1 1.1 pad_maximum_fusion.payload
  7.1 223.1 %shard_map.96 = (bf16[128,2048]{1,0:T(8,128)(2,1)}, bf16[128,2048]{1,0:T(8,128)(2,1)}, f32[256,2048]{1,0:T(8,128)}, f32[1,2048]{1,0:T(1,128)}) custom-call(bf16[128,2048]{1,0:T(8,128)(2,1)} %bitcast.15, bf16[128,2048]{1,0:T(8,128)(2,1)} %bitcast.16, bf16[128,2048]{1,0:T(8,128)(2,1)} %bitcast.12, bf16[4,272,512]{2,1,0:T(8,128)(2,1)} %pad_maximum_fusion.payload), custom_call_target="tpu_custom_call" | custom-call | tf_op jit(solution)/shard_map/pallas_call | solution.py:421
  230.2 0.0 copy-start
  230.2 1.4 constant_dynamic-slice_fusion
  231.6 1.9 copy.15
  233.5 1.9 copy.16
  235.4 0.0 copy-done
  235.4 1.3 copy.17
  (2 shorter events, 0.0 us)
Async XLA Ops:
  230.2 5.2 %copy-start = (f32[256,2048]{1,0:T(8,128)S(1)}, f32[256,2048]{1,0:T(8,128)}, u32[]{:S(2)}) copy-start(f32[256,2048]{1,0:T(8,128)} %get-tuple-element.10) | copy-start | bytes 6291460

commit v3 on v2

--- a/solution.py
+++ b/solution.py
@@ -35,8 +35,8 @@
 
 
 class Spread:
-    def __init__(self, buf, count, sems):
-        self.buf, self.count = buf, count
+    def __init__(self, buf, count, sems, paired):
+        self.buf, self.count, self.paired = buf, count, paired
         self.chain_s, self.chain_r, self.pair_s, self.pair_r = sems
         here = lax.axis_index("dp")
         self.place, self.side = here // 2, lax.rem(here, 2)
@@ -91,6 +91,8 @@
                 def _():
                     self.chain(layer, step, way).start()
 
+            if not self.paired:
+                continue
             if step == 0:
                 if way == 0:
                     self.pair(layer, 0, 0, self.side).start()
@@ -108,7 +110,8 @@
                     self.pair(layer, step, way, 1 - self.side).wait_recv()
 
     def drain(self, layer):
-        self.pair(layer, 0, 0, self.side).wait_send()
+        if self.paired:
+            self.pair(layer, 0, 0, self.side).wait_send()
         for step in range(self.count):
             for way in (0, 1):
                 if step < self.count - 1:
@@ -116,7 +119,7 @@
                     def _():
                         self.chain(layer, step, way).wait_send()
 
-                if step > 0:
+                if step > 0 and self.paired:
                     @pl.when(self.holds(step, way))
                     def _():
                         self.pair(layer, step, way, self.side).wait_send()
@@ -125,9 +128,9 @@
 def cascade_kernel(
     n, nd, micro, x_enc, x_dec, d_last, payload,
     out_ref, din_ref, grad_ref, dg_ref,
-    weights, dq_all, nq_own, nq_all, gain, y_buf, x_one, p_send, p_recv, d_own, d_recv, q_buf, g_send, g_recv,
-    y_ss, y_rs, p_ss, p_rs, d_ss, d_rs, g_ss, g_rs, a_ss, a_rs, n_ss, n_rs,
-    wz_s, wz_r, wy_s, wy_r, qz_s, qz_r, qy_s, qy_r,
+    weights, dq_all, nq_own, nq_all, gain, y_buf, x_one, p_send, p_recv, d_own, d_recv, q_buf, g_send, g_recv, g_part, h_send, h_recv,
+    y_ss, y_rs, p_ss, p_rs, d_ss, d_rs, g_ss, g_rs, a_ss, a_rs, n_ss, n_rs, h_ss, h_rs,
+    wz_s, wz_r, wy_s, wy_r, qz_s, qz_r,
 ):
     rows, features = x_enc.shape
     seq = rows // micro
@@ -141,7 +144,10 @@
     mine = pl.ds(pl.multiple_of(me * width, width), width)
     peers = [lax.rem(me + k, n) for k in range(1, n)]
     behind = [lax.rem(me + n - k, n) for k in range(1, n)]
-    dp_peers = [lax.rem(here + k, nd) for k in range(1, nd)]
+    place, side = here // 2, lax.rem(here, 2)
+    places = [lax.rem(place + k, half) for k in range(1, half)]
+    other = place * 2 + 1 - side
+    dp_peers = [p * 2 + side for p in places] + [other]
 
     def cols(j):
         return slice(j * width, (j + 1) * width)
@@ -151,7 +157,7 @@
         pl.semaphore_signal(barrier, inc=1, device_id={"section": peer}, device_id_type=MESH)
     for peer in dp_peers:
         pl.semaphore_signal(barrier, inc=1, device_id={"dp": peer}, device_id_type=MESH)
-    pl.semaphore_wait(barrier, n - 1 + nd - 1)
+    pl.semaphore_wait(barrier, n - 1 + half)
 
     def describe(src, dst, send, recv, peer, axis="section"):
         return pltpu.make_async_remote_copy(
@@ -165,8 +171,8 @@
         return copy
 
     pending = []
-    w_spread = Spread(weights, half, (wz_s, wz_r, wy_s, wy_r))
-    q_spread = Spread(dq_all, half, (qz_s, qz_r, qy_s, qy_r))
+    w_spread = Spread(weights, half, (wz_s, wz_r, wy_s, wy_r), True)
+    q_spread = Spread(dq_all, half, (qz_s, qz_r, None, None), False)
 
     for k, peer in enumerate(peers):
         pending.append(
@@ -267,30 +273,45 @@
 
     nq_copies = []
     for layer in range(n - 1, -1, -1):
-        for k, peer in enumerate(dp_peers):
+        for k, to in enumerate(places):
             nq_copies.append(
                 push(
-                    nq_own.at[layer, peer], nq_all.at[layer, here],
-                    n_ss.at[layer, k], n_rs.at[layer, k], peer, "dp",
+                    nq_own.at[layer, pl.ds(to * 2, 2)], nq_all.at[layer, place],
+                    n_ss.at[layer, k], n_rs.at[layer, k], to * 2 + side, "dp",
                 )
             )
-        nq_all[layer, here] = nq_own[layer, here]
+        nq_all[layer, place] = nq_own[layer, pl.ds(place * 2, 2)]
 
     def query_clock(clock):
         for i in range(n):
             if 0 <= clock - i < half:
                 q_spread.pump(n - 1 - i, clock - i)
 
-    def gradient(layer):
-        q_spread.finish(layer)
+    pair_copies = [
+        describe(h_send.at[layer], h_recv.at[layer], h_ss.at[layer], h_rs.at[layer], other, "dp")
+        for layer in range(n)
+    ]
+
+    def half_gradient(layer):
         i = n - 1 - layer
-        for copy in nq_copies[i * (nd - 1) : (i + 1) * (nd - 1)]:
+        for copy in nq_copies[i * (half - 1) : (i + 1) * (half - 1)]:
             copy.wait_recv()
-        left = nq_all[layer].reshape(nd * rows, depth)
-        right = jnp.concatenate([dq_all[layer, b, :rows, :] for b in range(nd)], axis=0)
-        g_send[layer, :depth, :] = dot(left, right, 0, 0).astype(BF16)
-        total = sum(dq_all[layer, b, rows : rows + PAD, :].astype(F32) for b in range(nd))
-        g_send[layer, depth:, :] = total.astype(BF16)
+        right = jnp.concatenate([dq_all[layer, c * 2 + side, :rows, :] for c in range(half)], axis=0)
+        total = sum(dq_all[layer, c * 2 + side, rows:, :].astype(F32) for c in range(half))
+
+        def product(to):
+            left = jnp.concatenate([nq_all[layer, c, to] for c in range(half)], axis=0)
+            return dot(left, right, 0, 0)
+
+        h_send[layer, :depth, :] = product(1 - side).astype(BF16)
+        h_send[layer, depth:, :] = total.astype(BF16)
+        pair_copies[layer].start()
+        g_part[layer, :depth, :] = product(side)
+        g_part[layer, depth:, :] = total
+
+    def whole_gradient(layer):
+        pair_copies[layer].wait_recv()
+        g_send[layer] = (g_part[layer] + h_recv[layer].astype(F32)).astype(BF16)
         deliver(g_send, g_recv, g_ss, g_rs, layer)
 
     def to_layer(buf, landing, send, recv, layer):
@@ -390,17 +411,19 @@
     for clock in range(n, n + half):
         query_clock(clock)
         while done < n and done + half - 1 <= clock:
-            if done == n - 1:
-                collect(d_own, d_recv, d_ss, d_rs)
-                for j in range(n):
-                    din_ref[:, cols(j)] = d_recv[j]
-            gradient(n - 1 - done)
+            half_gradient(n - 1 - done)
+            if done > 0:
+                whole_gradient(n - done)
             done += 1
+    collect(d_own, d_recv, d_ss, d_rs)
+    for j in range(n):
+        din_ref[:, cols(j)] = d_recv[j]
+    whole_gradient(0)
     collect(g_send, g_recv, g_ss, g_rs)
     for j in range(n):
         grad_ref[:, cols(j)] = g_recv[j, :depth, :].astype(F32)
         dg_ref[:, cols(j)] = g_recv[j, depth : depth + PAD, :][0:1].astype(F32)
-    for copy in pending + nq_copies:
+    for copy in pending + nq_copies + pair_copies:
         copy.wait_send()
     for layer in range(n):
         w_spread.drain(layer)
@@ -432,7 +455,7 @@
             pltpu.VMEM((n, nd, depth + PAD, width), BF16),
             pltpu.VMEM((n, nd, rows + PAD, width), BF16),
             pltpu.VMEM((n, nd, rows, depth), BF16),
-            pltpu.VMEM((n, nd, rows, depth), BF16),
+            pltpu.VMEM((n, half, 2, rows, depth), BF16),
             pltpu.VMEM((n, n, PAD, width), BF16),
             pltpu.VMEM((n, n, rows, width), BF16),
             pltpu.VMEM((n, rows, width), BF16),
@@ -443,17 +466,20 @@
             pltpu.VMEM((n, rows, width), BF16),
             pltpu.VMEM((n, depth + PAD, width), BF16),
             pltpu.VMEM((n, depth + PAD, width), BF16),
+            pltpu.VMEM((n, depth + PAD, width), F32),
+            pltpu.VMEM((n, depth + PAD, width), BF16),
+            pltpu.VMEM((n, depth + PAD, width), BF16),
             dma((n, n - 1)), dma((n, n - 1)),
             dma((n, n - 1)), dma((n, n - 1)),
             dma((n,)), dma((n,)),
             dma((n,)), dma((n,)),
             dma((n - 1,)), dma((n,)),
-            dma((n, nd - 1)), dma((n, nd - 1)),
-        ]
-        + [
+            dma((n, half - 1)), dma((n, half - 1)),
+            dma((n,)), dma((n,)),
             dma((2, n, half)), dma((2, n, half)),
             dma((n, 2 * half)), dma((n, 2 * half)),
-        ] * 2,
+            dma((2, n, half)), dma((2, n, half)),
+        ],
         compiler_params=pltpu.CompilerParams(
             collective_id=0, has_side_effects=True, vmem_limit_bytes=56 * 1024 * 1024
         ),

time: 237 us -> 245 us (1.034)
  Pallas kernels: 223 us -> 231 us
    pallas_call x1, Pallas kernels: 223 us -> 231 us  [cascade(): pl.pallas_call(functools.partial(cascade_kernel, n, nd, micro), out_shape...]
where the time goes in v3:
time: 245 us
  Pallas kernels  231 us (94%)
  local copies, waits for them, and re-layouts  8.5 us (3%)
  other arithmetic  4.46 us (2%)
    pallas_call x1, Pallas kernels, cascade(): pl.pallas_call(functools.partial(cascade_kernel, n, nd, micro), out_shape...  231 us
    unnamed x6, local copies, waits for them, and re-layouts  6.56 us

profile of v3, /device:TPU:0, one launch (start us, length us, event | category | flops | bytes accessed | tf_op | source)
XLA Modules:
  0.0 245.0 jit_solution(18266265891358844451)
XLA Ops:
  0.6 0.7 iota_compare_fusion
  1.4 0.7 reduce
  2.1 1.9 broadcast_select_fusion
  4.0 1.5 copy.10
  5.5 0.5 copy.11
  6.1 1.1 pad_maximum_fusion.payload
  7.1 231.4 %shard_map.96 = (bf16[128,2048]{1,0:T(8,128)(2,1)}, bf16[128,2048]{1,0:T(8,128)(2,1)}, f32[256,2048]{1,0:T(8,128)}, f32[1,2048]{1,0:T(1,128)}) custom-call(bf16[128,2048]{1,0:T(8,128)(2,1)} %bitcast.15, bf16[128,2048]{1,0:T(8,128)(2,1)} %bitcast.16, bf16[128,2048]{1,0:T(8,128)(2,1)} %bitcast.12, bf16[4,272,512]{2,1,0:T(8,128)(2,1)} %pad_maximum_fusion.payload), custom_call_target="tpu_custom_call" | custom-call | tf_op jit(solution)/shard_map/pallas_call | solution.py:444
  238.5 0.0 copy-start
  238.5 1.4 constant_dynamic-slice_fusion
  239.9 1.9 copy.15
  241.8 1.9 copy.16
  243.7 0.0 copy-done
  243.7 1.3 copy.17
  (2 shorter events, 0.0 us)
Async XLA Ops:
  238.5 5.2 %copy-start = (f32[256,2048]{1,0:T(8,128)S(1)}, f32[256,2048]{1,0:T(8,128)}, u32[]{:S(2)}) copy-start(f32[256,2048]{1,0:T(8,128)} %get-tuple-element.10) | copy-start | bytes 6291460

commit v4 on v2

--- a/solution.py
+++ b/solution.py
@@ -206,6 +206,7 @@
     def own_source(layer):
         return x_enc[:, mine] if layer == 0 else y_buf[0, me]
 
+    nq_copies = [None] * n
     inv_in = [None] * n
     inv_src = [None] * n
 
@@ -258,6 +259,14 @@
             push(y_buf.at[layer, me], y_buf.at[layer, me], y_ss.at[layer, k], y_rs.at[layer, k], peer)
             for k, peer in enumerate(peers)
         ]
+        nq_copies[layer] = [
+            push(
+                nq_own.at[layer, peer], nq_all.at[layer, here],
+                n_ss.at[layer, k], n_rs.at[layer, k], peer, "dp",
+            )
+            for k, peer in enumerate(dp_peers)
+        ]
+        nq_all[layer, here] = nq_own[layer, here]
         if layer < n - 1:
             for copy in copies:
                 copy.wait_recv()
@@ -265,17 +274,6 @@
             last = copies
         pending += copies
 
-    nq_copies = []
-    for layer in range(n - 1, -1, -1):
-        for k, peer in enumerate(dp_peers):
-            nq_copies.append(
-                push(
-                    nq_own.at[layer, peer], nq_all.at[layer, here],
-                    n_ss.at[layer, k], n_rs.at[layer, k], peer, "dp",
-                )
-            )
-        nq_all[layer, here] = nq_own[layer, here]
-
     def query_clock(clock):
         for i in range(n):
             if 0 <= clock - i < half:
@@ -283,8 +281,7 @@
 
     def gradient(layer):
         q_spread.finish(layer)
-        i = n - 1 - layer
-        for copy in nq_copies[i * (nd - 1) : (i + 1) * (nd - 1)]:
+        for copy in nq_copies[layer]:
             copy.wait_recv()
         left = nq_all[layer].reshape(nd * rows, depth)
         right = jnp.concatenate([dq_all[layer, b, :rows, :] for b in range(nd)], axis=0)
@@ -400,7 +397,7 @@
     for j in range(n):
         grad_ref[:, cols(j)] = g_recv[j, :depth, :].astype(F32)
         dg_ref[:, cols(j)] = g_recv[j, depth : depth + PAD, :][0:1].astype(F32)
-    for copy in pending + nq_copies:
+    for copy in pending + sum(nq_copies, []):
         copy.wait_send()
     for layer in range(n):
         w_spread.drain(layer)

time: 237 us -> 237 us (level)
  no operation moved by 1% of the time
where the time goes in v4:
time: 237 us; the launch traced here: 236 us
  Pallas kernels  223 us (94%)
  local copies, waits for them, and re-layouts  8.5 us (4%)
  other arithmetic  4.46 us (2%)
    pallas_call x1, Pallas kernels, cascade(): pl.pallas_call(functools.partial(cascade_kernel, n, nd, micro), out_shape...  223 us
    unnamed x6, local copies, waits for them, and re-layouts  6.56 us

profile of v4, /device:TPU:0, one launch (start us, length us, event | category | flops | bytes accessed | tf_op | source)
XLA Modules:
  0.0 236.2 jit_solution(15251738529137531976)
XLA Ops:
  0.6 0.7 iota_compare_fusion
  1.4 0.7 reduce
  2.1 1.9 broadcast_select_fusion
  4.0 1.5 copy.10
  5.5 0.5 copy.11
  6.1 1.1 pad_maximum_fusion.payload
  7.1 222.5 %shard_map.96 = (bf16[128,2048]{1,0:T(8,128)(2,1)}, bf16[128,2048]{1,0:T(8,128)(2,1)}, f32[256,2048]{1,0:T(8,128)}, f32[1,2048]{1,0:T(1,128)}) custom-call(bf16[128,2048]{1,0:T(8,128)(2,1)} %bitcast.15, bf16[128,2048]{1,0:T(8,128)(2,1)} %bitcast.16, bf16[128,2048]{1,0:T(8,128)(2,1)} %bitcast.12, bf16[4,272,512]{2,1,0:T(8,128)(2,1)} %pad_maximum_fusion.payload), custom_call_target="tpu_custom_call" | custom-call | tf_op jit(solution)/shard_map/pallas_call | solution.py:418
  229.7 0.0 copy-start
  229.7 1.4 constant_dynamic-slice_fusion
  231.1 1.9 copy.15
  233.0 1.9 copy.16
  234.9 0.0 copy-done
  234.9 1.3 copy.17
  (2 shorter events, 0.0 us)
Async XLA Ops:
  229.7 5.2 %copy-start = (f32[256,2048]{1,0:T(8,128)S(1)}, f32[256,2048]{1,0:T(8,128)}, u32[]{:S(2)}) copy-start(f32[256,2048]{1,0:T(8,128)} %get-tuple-element.10) | copy-start | bytes 6291460
